TPU v7x, 256 devices: a whole 4x4x8 slice. The times are simulated.
256 devices in a mesh: seq: 32 (over z, y), head: 8 (over x, core).
Axes of the slice: x: 4, y: 4, z: 8, core: 2. Of those that a mesh axis runs over, the one named last changes fastest.
Arguments:
- queries: bfloat16 [16384, 7168], P('seq', 'head'), may hold values from -140 to 140
- keys: bfloat16 [16384, 7168], P('seq', 'head'), may hold values from -7 to 7
- values: bfloat16 [16384, 7168], P('seq', 'head'), may hold values from -6 to 6
- out_grad: bfloat16 [16384, 7168], P(('seq', 'head')), may hold values from -6 to 6
- selection: int32 [512, 3], replicated, may hold values from 0 to 31, as said below
Outputs:
- query_grad: bfloat16 [16384, 7168], P('seq', 'head')
- key_grad: bfloat16 [16384, 7168], P('seq', 'head')
- value_grad: bfloat16 [16384, 7168], P('seq', 'head')
Inputs may be any that keep to these rules, and one draw needn't show every extreme that they name: `selection`: row c lists the key blocks selected by query stretch c, whose own block is c // 16. An entry equal to the own block selects nothing; every other entry names an earlier block, and the entries of a row that select something are distinct. The 16 stretches of one own block together name each earlier block at most once, and name block 0 exactly once when their own block is not 0.
All inputs are finite; a program needn't handle non-finite values.
Results may differ from a plain program's by a relative error of at most 0.0065.
Values may be sent and summed in bfloat16 or wider, within the bound.
A program may use at most 128 MiB of HBM per device.

v0:
```python
import functools
import math

import jax
import jax.numpy as jnp
from jax import lax
from jax.experimental import pallas as pl
from jax.experimental.pallas import tpu as pltpu
from jax.sharding import PartitionSpec as P

HD = 128
QCHUNK = 32
TILE_SLOTS = 8
TILE = TILE_SLOTS * QCHUNK
GROUP = 128 // QCHUNK
PIECES = 4
SCALE = 1.0 / math.sqrt(HD)
EXPO = SCALE * math.log2(math.e)
NEG = -1e30
BIG = 1e30
NT_DIMS = (((1,), (1,)), ((), ()))
MESH = pl.DeviceIdType.MESH


def head_chunks(head_count):
    edges = list(range(0, head_count, 2)) + [head_count]
    return tuple(zip(edges[:-1], edges[1:]))


def dot(lhs, rhs):
    return jnp.dot(lhs, rhs, preferred_element_type=jnp.float32)


def dot_nt(lhs, rhs):
    return lax.dot_general(lhs, rhs, NT_DIMS, preferred_element_type=jnp.float32)


def score_columns(key_tile, query_tile, diagonal):
    scores = dot_nt(key_tile, query_tile)
    if diagonal is not None:
        rows = lax.broadcasted_iota(jnp.int32, scores.shape, 0)
        cols = lax.broadcasted_iota(jnp.int32, scores.shape, 1)
        scores = jnp.where(rows <= cols + diagonal, scores, NEG)
    return scores


def stats_tile(key_tile, value_tile, query_tile, grad_tile, diagonal, weight_ref, prob_ref, top_ref):
    scores = score_columns(key_tile, query_tile, diagonal)
    grad_prob = dot_nt(value_tile, grad_tile)
    prob_ref[...] = grad_prob
    rows = scores.shape[0] // PIECES
    tops, totals, inners = [], [], []
    for piece in range(PIECES):
        span = slice(piece * rows, piece * rows + rows)
        top = jnp.max(scores[span], axis=0, keepdims=True)
        weights = jnp.exp2((scores[span] - top) * EXPO)
        weight_ref[span] = weights
        top_ref[piece : piece + 1] = top
        tops.append(top)
        totals.append(jnp.sum(weights, axis=0, keepdims=True))
        inners.append(jnp.sum(weights * grad_prob[span], axis=0, keepdims=True))
    best = functools.reduce(jnp.maximum, tops)
    factors = [jnp.exp2((top - best) * EXPO) for top in tops]
    total = sum(factor * part for factor, part in zip(factors, totals))
    inner = sum(factor * part for factor, part in zip(factors, inners))
    return best, total, inner


def grads_tile(key_t, query_tile, grad_tile, log_row, delta_row, weight_ref, prob_ref, top_ref):
    rows = weight_ref.shape[0] // PIECES
    probs, scores = [], []
    for piece in range(PIECES):
        span = slice(piece * rows, piece * rows + rows)
        prob = weight_ref[span] * jnp.exp2((top_ref[piece : piece + 1] - log_row) * EXPO)
        probs.append(prob.astype(jnp.bfloat16))
        scores.append((prob * (prob_ref[span] - delta_row)).astype(jnp.bfloat16))
    prob_half = jnp.concatenate(probs, axis=0)
    grad_score = jnp.concatenate(scores, axis=0)
    grad_key = dot(grad_score, query_tile)
    grad_value = dot(prob_half, grad_tile)
    grad_query = dot(key_t, grad_score).T
    return grad_query, grad_key, grad_value


def quarter_swap(parts, target):
    lane = lax.broadcasted_iota(jnp.int32, parts[0].shape, 1) // QCHUNK
    out = jnp.zeros(parts[0].shape, jnp.float32)
    for source, part in enumerate(parts):
        shift = ((source - target) * QCHUNK) % 128
        moved = pltpu.roll(part, shift, 1) if shift else part
        out = jnp.where(lane == source, moved, out)
    return out


def kernel(n, nh, heads, chunks, *refs):
    refs = list(refs)
    sent_stretch, sent_used, own_pick, own_live = refs[:4]
    q_ref, k_ref, v_ref, g_ref = refs[4:8]
    dq_ref, dk_ref, dv_ref = refs[8:11]
    g_own, k_t, dk_acc, dv_acc, dq_own = refs[11:16]
    stat_far, stat_own, own_rows, far_rows, logs_own, log_far, delta_far, log_head, delta_head = refs[16:25]
    head_send, head_recv = refs[25:27]
    far_kept, high_kept, low_kept = refs[27:30], refs[30:33], refs[33:36]
    rest = refs[36:]
    buffers = []
    for _ in chunks:
        buffers.append(rest[:20])
        rest = rest[20:]

    me = lax.axis_index("seq")
    hx = lax.axis_index("head")
    stretches = q_ref.shape[0]
    block = stretches * QCHUNK
    feats = heads * HD
    piece = stretches // nh
    tiles = n // TILE_SLOTS
    first_tile = (me + 1) // TILE_SLOTS

    def head_cols(head):
        return pl.ds(pl.multiple_of(head * HD, HD), HD)

    barrier = pltpu.get_barrier_semaphore()

    def greet_seq(step, carry):
        peer = lax.rem(me + step, n)
        pl.semaphore_signal(barrier, inc=1, device_id=(peer, hx), device_id_type=MESH)
        return carry

    def greet_head(step, carry):
        peer = lax.rem(hx + step, nh)
        pl.semaphore_signal(barrier, inc=1, device_id=(me, peer), device_id_type=MESH)
        return carry

    lax.fori_loop(1, n, greet_seq, 0)
    lax.fori_loop(1, nh, greet_head, 0)
    pl.semaphore_wait(barrier, n - 1 + nh - 1)

    def head_copy(peer, slot):
        return pltpu.make_async_remote_copy(
            src_ref=g_ref.at[:, :, pl.ds(pl.multiple_of(peer * feats, HD), feats)],
            dst_ref=g_own.at[pl.ds(slot * piece, piece)],
            send_sem=head_send.at[peer],
            recv_sem=head_recv.at[slot],
            device_id=(me, peer),
            device_id_type=MESH,
        )

    def start_head(step, carry):
        head_copy(lax.rem(hx + step, nh), hx).start()
        return carry

    lax.fori_loop(1, nh, start_head, 0)

    def pair_copy(src, dst, send, recv, peer, slot):
        return pltpu.make_async_remote_copy(
            src_ref=src.at[peer],
            dst_ref=dst.at[slot],
            send_sem=send.at[peer],
            recv_sem=recv.at[slot],
            device_id=(peer, hx),
            device_id_type=MESH,
        )

    def mixed(i):
        return lax.rem(i * 13, n - 1) + 1

    def each_near(body):
        def step(i, carry):
            shift = mixed(i)

            @pl.when(shift <= me)
            def _():
                body(me - shift)

            return carry

        lax.fori_loop(0, n - 1, step, 0)

    def each_far(body):
        def step(i, carry):
            shift = mixed(i)

            @pl.when(me + shift < n)
            def _():
                body(me + shift)

            return carry

        lax.fori_loop(0, n - 1, step, 0)

    def send_rows(source, src, dst, send, recv, start, stop):
        def body(peer):
            row = sent_stretch[peer]
            for head in range(start, stop):
                src[peer, head - start] = source[row, :, head * HD : head * HD + HD]
            pair_copy(src, dst, send, recv, peer, me).start()

        each_near(body)

    def wait_far(src, dst, send, recv):
        def step(peer, carry):
            pair_copy(src, dst, send, recv, peer, peer).wait_recv()
            return carry

        lax.fori_loop(me + 1, n, step, 0)

    def wait_near(src, dst, send, recv):
        def step(peer, carry):
            pair_copy(src, dst, send, recv, peer, peer).wait_recv()
            return carry

        lax.fori_loop(0, me, step, 0)

    def sent_down(src, dst, send, recv):
        def step(peer, carry):
            pair_copy(src, dst, send, recv, peer, me).wait_send()
            return carry

        lax.fori_loop(0, me, step, 0)

    def start_up(src, dst, send, recv):
        each_far(lambda peer: pair_copy(src, dst, send, recv, peer, me).start())

    def sent_up(src, dst, send, recv):
        def step(peer, carry):
            pair_copy(src, dst, send, recv, peer, me).wait_send()
            return carry

        lax.fori_loop(me + 1, n, step, 0)

    groups = []
    for held in buffers:
        groups.append(tuple(tuple(held[4 * i : 4 * i + 4]) for i in range(5)))

    for index in range(2):
        send_rows(q_ref, *groups[index][0], *chunks[index])

    def clear(slot, carry):
        for rows, grads, stats, logs, parts in groups:
            rows[1][slot] = jnp.zeros(rows[1].shape[1:], jnp.bfloat16)
            grads[1][slot] = jnp.zeros(grads[1].shape[1:], jnp.bfloat16)
            logs[1][slot, 0:1] = jnp.full((1, 128), BIG, jnp.float32)
            logs[1][slot, 1:2] = jnp.zeros((1, 128), jnp.float32)
        return carry

    lax.fori_loop(0, me + 1, clear, 0)

    def turn(head, carry):
        k_t[head] = k_ref[:, head_cols(head)].T
        return carry

    lax.fori_loop(0, heads, turn, 0)

    g_own[pl.ds(hx * piece, piece)] = g_ref[:, :, pl.ds(pl.multiple_of(hx * feats, HD), feats)]

    def wait_head(step, carry):
        peer = lax.rem(hx + step, nh)
        head_copy(peer, peer).wait_recv()
        return carry

    lax.fori_loop(1, nh, wait_head, 0)
    send_rows(g_own, *groups[0][1], *chunks[0])

    half = block // 2
    middle = stretches // 2

    def own_tile(source, upper, cols):
        places = slice(middle, stretches) if upper else slice(0, middle)
        return source[places, :, cols].reshape(half, HD)

    def pad_stats(top, total, inner):
        return jnp.concatenate([top, total, inner, jnp.zeros((5, top.shape[1]), jnp.float32)], axis=0)

    def own_stats(head, carry):
        cols = head_cols(head)
        stat_own[head, :, 0:half] = pad_stats(
            *stats_tile(
                k_ref[0:half, cols], v_ref[0:half, cols], own_tile(q_ref, False, cols), own_tile(g_own, False, cols), 0,
                *(kept.at[head] for kept in low_kept),
            )
        )
        stat_own[head, :, half:block] = pad_stats(
            *stats_tile(
                k_ref[:, cols], v_ref[:, cols], own_tile(q_ref, True, cols), own_tile(g_own, True, cols), half,
                *(kept.at[head] for kept in high_kept),
            )
        )
        return carry

    lax.fori_loop(0, heads, own_stats, 0)

    def chunk_stats(chunk):
        (start, stop), (rows, grads, stats, logs, parts) = chunks[chunk], groups[chunk]
        count = stop - start
        wait_far(*rows)
        wait_far(*grads)

        def far_stats(tile, carry):
            slots = pl.ds(pl.multiple_of(tile * TILE_SLOTS, TILE_SLOTS), TILE_SLOTS)
            for local in range(count):
                cols = pl.ds((local + start) * HD, HD)
                query_tile = rows[1][slots, local].reshape(TILE, HD)
                grad_tile = grads[1][slots, local].reshape(TILE, HD)
                stat_far[local, :, pl.ds(pl.multiple_of(tile * TILE, TILE), TILE)] = pad_stats(
                    *stats_tile(
                        k_ref[:, cols], v_ref[:, cols], query_tile, grad_tile, None,
                        *(kept.at[chunk % 2, local, tile] for kept in far_kept),
                    )
                )
            return carry

        lax.fori_loop(first_tile, tiles, far_stats, 0)

        def far_swap(group, carry):
            lanes = pl.ds(pl.multiple_of(group * 128, 128), 128)
            held = [stat_far[local, :, lanes] for local in range(count)]
            for slot in range(GROUP):
                stats[0][group * GROUP + slot] = quarter_swap(held, slot)
            return carry

        lax.fori_loop(first_tile * (TILE // 128), n // GROUP, far_swap, 0)
        start_up(*stats)

    def chunk_logs(chunk):
        (start, stop), (rows, grads, stats, logs, parts) = chunks[chunk], groups[chunk]
        count = stop - start
        for group in range(stretches // GROUP):
            held = [stat_own[start + local, :, group * 128 : group * 128 + 128] for local in range(count)]
            for slot in range(GROUP):
                swapped = quarter_swap(held, slot)
                row = group * GROUP + slot
                for kind in range(3):
                    own_rows[kind, row : row + 1] = swapped[kind : kind + 1]

        wait_near(*stats)
        fill = jnp.where(lax.broadcasted_iota(jnp.int32, (8, 128), 0) == 0, NEG, 0.0)
        for row in range(stretches):
            for pick in range(3):
                live = own_live[row * 3 + pick]
                found = jnp.where(jnp.full((8, 128), live, jnp.int32) > 0, stats[1][own_pick[row * 3 + pick]], fill)
                for kind in range(3):
                    far_rows[pick, kind, row : row + 1] = found[kind : kind + 1]
        best = own_rows[0]
        for pick in range(3):
            best = jnp.maximum(best, far_rows[pick, 0])
        weight = jnp.exp2((own_rows[0] - best) * EXPO)
        total = own_rows[1] * weight
        inner = own_rows[2] * weight
        for pick in range(3):
            weight = jnp.exp2((far_rows[pick, 0] - best) * EXPO)
            total += far_rows[pick, 1] * weight
            inner += far_rows[pick, 2] * weight
        log_total = best + (jnp.log(total) - math.log(SCALE)) * (1.0 / SCALE)
        delta = inner / total
        for row in range(stretches):
            logs_own[row, 0:1] = log_total[row : row + 1]
            logs_own[row, 1:2] = delta[row : row + 1]

        def send_logs(peer):
            row = sent_stretch[peer]
            used = jnp.full((1, 128), sent_used[peer], jnp.int32) > 0
            logs[0][peer, 0:1] = jnp.where(used, logs_own[row, 0:1], BIG)
            logs[0][peer, 1:2] = jnp.where(used, logs_own[row, 1:2], 0.0)
            pair_copy(*logs, peer, me).start()

        each_near(send_logs)

        for group in range(stretches // GROUP):
            for kind, kept in ((0, log_head), (1, delta_head)):
                lines = [
                    jnp.broadcast_to(logs_own[group * GROUP + slot, kind : kind + 1], (8, 128))
                    for slot in range(GROUP)
                ]
                for local in range(count):
                    kept[local, :, group * 128 : group * 128 + 128] = quarter_swap(lines, local)

    def chunk_own(chunk):
        (start, stop), (rows, grads, stats, logs, parts) = chunks[chunk], groups[chunk]
        count = stop - start
        def own_grads(local, carry):
            head = local + start
            cols = head_cols(head)
            grad_query, grad_key, grad_value = grads_tile(
                k_t[head], own_tile(q_ref, True, cols), own_tile(g_own, True, cols),
                log_head[local, 0:1, half:block], delta_head[local, 0:1, half:block],
                *(kept.at[head] for kept in high_kept),
            )
            dq_own[head, half:block] = grad_query
            dk_acc[head] = grad_key
            dv_acc[head] = grad_value
            grad_query, grad_key, grad_value = grads_tile(
                k_t[head, :, 0:half], own_tile(q_ref, False, cols), own_tile(g_own, False, cols),
                log_head[local, 0:1, 0:half], delta_head[local, 0:1, 0:half],
                *(kept.at[head] for kept in low_kept),
            )
            dq_own[head, 0:half] = grad_query
            dk_acc[head, 0:half] += grad_key
            dv_acc[head, 0:half] += grad_value
            return carry

        lax.fori_loop(0, count, own_grads, 0)

    def chunk_far(chunk):
        (start, stop), (rows, grads, stats, logs, parts) = chunks[chunk], groups[chunk]
        count = stop - start
        wait_far(*logs)

        def far_logs(group, carry):
            lanes = pl.ds(pl.multiple_of(group * 128, 128), 128)
            for kind, kept in ((0, log_far), (1, delta_far)):
                lines = [
                    jnp.broadcast_to(logs[1][group * GROUP + slot, kind : kind + 1], (8, 128)) for slot in range(GROUP)
                ]
                for local in range(count):
                    kept[local, :, lanes] = quarter_swap(lines, local)
            return carry

        lax.fori_loop(first_tile * (TILE // 128), n // GROUP, far_logs, 0)

        def far_grads(tile, carry):
            slots = pl.ds(pl.multiple_of(tile * TILE_SLOTS, TILE_SLOTS), TILE_SLOTS)
            lanes = pl.ds(pl.multiple_of(tile * TILE, TILE), TILE)
            for local in range(count):
                head = local + start
                query_tile = rows[1][slots, local].reshape(TILE, HD)
                grad_tile = grads[1][slots, local].reshape(TILE, HD)
                grad_query, grad_key, grad_value = grads_tile(
                    k_t[head], query_tile, grad_tile, log_far[local, 0:1, lanes], delta_far[local, 0:1, lanes],
                    *(kept.at[chunk % 2, local, tile] for kept in far_kept),
                )
                parts[0][slots, local] = grad_query.astype(jnp.bfloat16).reshape(TILE_SLOTS, QCHUNK, HD)
                dk_acc[head] += grad_key
                dv_acc[head] += grad_value
            return carry

        lax.fori_loop(first_tile, tiles, far_grads, 0)
        start_up(*parts)

    last = len(chunks)
    for chunk in range(last):
        chunk_stats(chunk)
        if chunk + 1 < last:
            send_rows(g_own, *groups[chunk + 1][1], *chunks[chunk + 1])
        if chunk + 2 < last:
            send_rows(q_ref, *groups[chunk + 2][0], *chunks[chunk + 2])
        if chunk > 0:
            chunk_far(chunk - 1)
        chunk_logs(chunk)
        chunk_own(chunk)
    chunk_far(last - 1)

    def write_keys(head, carry):
        cols = head_cols(head)
        dk_ref[:, cols] = dk_acc[head].astype(jnp.bfloat16)
        dv_ref[:, cols] = (dv_acc[head] * math.sqrt(HD)).astype(jnp.bfloat16)
        return carry

    lax.fori_loop(0, heads, write_keys, 0)

    def all_sent():
        def head_sent(step, carry):
            head_copy(lax.rem(hx + step, nh), hx).wait_send()
            return carry

        lax.fori_loop(1, nh, head_sent, 0)
        for rows, grads, stats, logs, parts in groups:
            sent_down(*rows)
            sent_down(*grads)
            sent_up(*stats)
            sent_down(*logs)
            sent_up(*parts)

    def chunk_queries(chunk):
        (start, stop), parts = chunks[chunk], groups[chunk][4]
        wait_near(*parts)

        def write_queries(row, carry):
            place = pl.ds(pl.multiple_of(row * QCHUNK, QCHUNK), QCHUNK)
            for local in range(stop - start):
                total = dq_own[start + local, place]
                for pick in range(3):
                    live = jnp.full((QCHUNK, HD), own_live[row * 3 + pick], jnp.int32) > 0
                    far = parts[1][own_pick[row * 3 + pick], local].astype(jnp.float32)
                    total += jnp.where(live, far, 0.0)
                dq_ref[place, pl.ds((start + local) * HD, HD)] = total.astype(jnp.bfloat16)
            return carry

        lax.fori_loop(0, stretches, write_queries, 0)

    for chunk in range(last - 1):
        chunk_queries(chunk)
    all_sent()
    chunk_queries(last - 1)


def attention_grads(n, nh, tables, queries, keys, values, out_grad):
    block, feats = queries.shape
    heads = feats // HD
    chunks = head_chunks(heads)
    stretches = block // QCHUNK
    bf, f32 = jnp.bfloat16, jnp.float32
    dma = pltpu.SemaphoreType.DMA
    most = max(stop - start for start, stop in chunks)
    scratch = [
        pltpu.VMEM((stretches, QCHUNK, feats), bf),
        pltpu.VMEM((heads, HD, block), bf),
        pltpu.VMEM((heads, block, HD), f32),
        pltpu.VMEM((heads, block, HD), f32),
        pltpu.VMEM((heads, block, HD), f32),
        pltpu.VMEM((most, 8, n * QCHUNK), f32),
        pltpu.VMEM((heads, 8, block), f32),
        pltpu.VMEM((3, stretches, 128), f32),
        pltpu.VMEM((3, 3, stretches, 128), f32),
        pltpu.VMEM((stretches, 2, 128), f32),
        pltpu.VMEM((most, 8, n * QCHUNK), f32),
        pltpu.VMEM((most, 8, n * QCHUNK), f32),
        pltpu.VMEM((most, 8, block), f32),
        pltpu.VMEM((most, 8, block), f32),
        dma((nh,)),
        dma((nh,)),
    ]
    half = block // 2
    for lead, keys_held, cols_held in (
        ((2, most, n // TILE_SLOTS), block, TILE),
        ((heads,), block, half),
        ((heads,), half, half),
    ):
        scratch += [pltpu.VMEM((*lead, rows, cols_held), f32) for rows in (keys_held, keys_held, 8)]
    for start, stop in chunks:
        row_shape = (n, stop - start, QCHUNK, HD)
        for shape, dtype in (
            (row_shape, bf),
            (row_shape, bf),
            ((n, 8, 128), f32),
            ((n, 2, 128), f32),
            (row_shape, bf),
        ):
            scratch += [pltpu.VMEM(shape, dtype), pltpu.VMEM(shape, dtype), dma((n,)), dma((n,))]
    whole = pl.BlockSpec(memory_space=pltpu.VMEM)
    small = pl.BlockSpec(memory_space=pltpu.SMEM)
    out = jax.ShapeDtypeStruct((block, feats), bf)
    pairs = (n + stretches) // 2 * QCHUNK * block * feats
    return pl.pallas_call(
        functools.partial(kernel, n, nh, heads, chunks),
        out_shape=(out, out, out),
        in_specs=[small] * 4 + [whole] * 4,
        out_specs=(whole, whole, whole),
        scratch_shapes=scratch,
        cost_estimate=pl.CostEstimate(flops=14 * pairs, bytes_accessed=14 * block * feats, transcendentals=0),
        compiler_params=pltpu.CompilerParams(
            collective_id=0, has_side_effects=True, vmem_limit_bytes=60 * 1024 * 1024
        ),
    )(*tables, queries.reshape(stretches, QCHUNK, feats), keys, values, out_grad.reshape(-1, QCHUNK, nh * feats))


def per_device(queries, keys, values, out_grad, selection):
    n = lax.axis_size("seq")
    nh = lax.axis_size("head")
    me = lax.axis_index("seq")
    stretches = queries.shape[0] // QCHUNK
    own = lax.dynamic_slice_in_dim(selection, me * stretches, stretches, 0)
    live = own != me
    peers = jnp.arange(n, dtype=jnp.int32)
    hits = (own[:, :, None] == peers[None, None, :]) & live[:, :, None]
    places = jnp.arange(stretches, dtype=jnp.int32)[:, None, None]
    used = jnp.any(hits, axis=(0, 1)).astype(jnp.int32)
    stretch = jnp.sum(jnp.where(hits, places, 0), axis=(0, 1))
    tables = (
        stretch,
        used,
        jnp.where(live, own, 0).reshape(-1),
        live.astype(jnp.int32).reshape(-1),
    )
    return attention_grads(n, nh, tables, queries, keys, values, out_grad)


def solution(mesh):
    return jax.shard_map(
        per_device,
        mesh=mesh,
        in_specs=(
            P("seq", "head"),
            P("seq", "head"),
            P("seq", "head"),
            P(("seq", "head"), None),
            P(),
        ),
        out_specs=(P("seq", "head"), P("seq", "head"), P("seq", "head")),
        check_vma=False,
    )
```

profile of v0, /device:TPU:64, one launch (start us, length us, event | category | flops | bytes accessed | tf_op | source)
XLA Modules:
  0.0 163.6 jit_solution(6996900258899157118)
XLA Ops:
  0.6 0.8 fusion.2
  1.4 0.1 fusion.1
  1.5 0.5 convert_element_type.4.refs_1_
  2.0 0.6 select_reduce_fusion.refs_0_
  2.6 0.1 copy.16
  2.7 0.6 reshape.22.refs_2_
  3.3 0.1 copy.17
  3.4 0.7 reshape.28.refs_3_
  4.1 154.9 %shard_map.76 = (bf16[512,896]{1,0:T(8,128)(2,1)}, bf16[512,896]{1,0:T(8,128)(2,1)}, bf16[512,896]{1,0:T(8,128)(2,1)}) custom-call(s32[32]{0:T(128)} %select_reduce_fusion.refs_0_, s32[32]{0:T(128)} %convert_element_type.4.refs_1_, s32[48]{0:T(128)} %reshape.22.refs_2_, s32[48]{0:T(128)} %reshape.28.refs_3_, bf16[16,32,896]{2,1,0:T(8,128)(2,1)} %bitcast.2, ...), custom_call_target="tpu_custom_call" | custom-call | flops 4932501504 | bytes 6422528 | tf_op jit(solution)/shard_map/pallas_call | solution.py:543
  158.9 0.0 copy-start.1
  158.9 2.3 %copy.21 = bf16[512,896]{1,0:T(8,128)(2,1)} copy(bf16[512,896]{1,0:T(8,128)(2,1)} %get-tuple-element.9) | data formatting | bytes 1835008
  161.2 0.0 copy-done.1
  161.2 0.0 copy-start
  161.2 0.9 copy.22
  162.1 0.6 copy-done
  162.7 0.9 copy.23
  (1 shorter events, 0.0 us)
Async XLA Ops:
  158.9 2.3 %copy-start.1 = (bf16[512,896]{1,0:T(8,128)(2,1)S(1)}, bf16[512,896]{1,0:T(8,128)(2,1)}, u32[]{:S(2)}) copy-start(bf16[512,896]{1,0:T(8,128)(2,1)} %get-tuple-element.10) | copy-start | bytes 2752516
  161.2 1.5 copy-start
where the time goes:
time: 164 us
  Pallas kernels  155 us (95%)
  local copies, waits for them, and re-layouts  6.13 us (4%)
  other arithmetic  1.99 us (1%)
    pallas_call x1, Pallas kernels, attention_grads(): pl.pallas_call(functools.partial(kernel, n, nh, heads, chunks), out_shape...  155 us
    unnamed x7, local copies, waits for them, and re-layouts  4.69 us

commit v1 on v0

--- a/solution.py
+++ b/solution.py
@@ -161,39 +161,34 @@
             device_id_type=MESH,
         )
 
-    def mixed(i):
-        return lax.rem(i * 13, n - 1) + 1
-
     def each_near(body):
         def step(i, carry):
-            shift = mixed(i)
-
-            @pl.when(shift <= me)
-            def _():
-                body(me - shift)
-
-            return carry
-
-        lax.fori_loop(0, n - 1, step, 0)
+            place = me - 1 - i
+            hop = place // 2
+            body(hop + (place % 2) * (me - 1 - 2 * hop))
+            return carry
+
+        lax.fori_loop(0, me, step, 0)
 
     def each_far(body):
         def step(i, carry):
-            shift = mixed(i)
-
-            @pl.when(me + shift < n)
-            def _():
-                body(me + shift)
-
-            return carry
-
-        lax.fori_loop(0, n - 1, step, 0)
-
-    def send_rows(source, src, dst, send, recv, start, stop):
+            place = n - 2 - me - i
+            hop = place // 2
+            body(n - 1 - hop - (place % 2) * (n - 2 - me - 2 * hop))
+            return carry
+
+        lax.fori_loop(0, n - 1 - me, step, 0)
+
+    def start_down(src, dst, send, recv):
+        each_near(lambda peer: pair_copy(src, dst, send, recv, peer, me).start())
+
+    def gather_rows(source, kind):
         def body(peer):
             row = sent_stretch[peer]
-            for head in range(start, stop):
-                src[peer, head - start] = source[row, :, head * HD : head * HD + HD]
-            pair_copy(src, dst, send, recv, peer, me).start()
+            for (start, stop), group in zip(chunks, groups):
+                for head in range(start, stop):
+                    group[kind][0][peer, head - start] = source[row, :, head * HD : head * HD + HD]
+            pair_copy(*groups[0][kind], peer, me).start()
 
         each_near(body)
 
@@ -232,8 +227,8 @@
     for held in buffers:
         groups.append(tuple(tuple(held[4 * i : 4 * i + 4]) for i in range(5)))
 
-    for index in range(2):
-        send_rows(q_ref, *groups[index][0], *chunks[index])
+    gather_rows(q_ref, 0)
+    start_down(*groups[1][0])
 
     def clear(slot, carry):
         for rows, grads, stats, logs, parts in groups:
@@ -259,7 +254,7 @@
         return carry
 
     lax.fori_loop(1, nh, wait_head, 0)
-    send_rows(g_own, *groups[0][1], *chunks[0])
+    gather_rows(g_own, 1)
 
     half = block // 2
     middle = stretches // 2
@@ -288,6 +283,14 @@
         return carry
 
     lax.fori_loop(0, heads, own_stats, 0)
+    for chunk, (start, stop) in enumerate(chunks):
+        for group in range(stretches // GROUP):
+            held = [stat_own[head, :, group * 128 : group * 128 + 128] for head in range(start, stop)]
+            for slot in range(GROUP):
+                swapped = quarter_swap(held, slot)
+                row = group * GROUP + slot
+                for kind in range(3):
+                    own_rows[chunk, kind, row : row + 1] = swapped[kind : kind + 1]
 
     def chunk_stats(chunk):
         (start, stop), (rows, grads, stats, logs, parts) = chunks[chunk], groups[chunk]
@@ -324,14 +327,6 @@
     def chunk_logs(chunk):
         (start, stop), (rows, grads, stats, logs, parts) = chunks[chunk], groups[chunk]
         count = stop - start
-        for group in range(stretches // GROUP):
-            held = [stat_own[start + local, :, group * 128 : group * 128 + 128] for local in range(count)]
-            for slot in range(GROUP):
-                swapped = quarter_swap(held, slot)
-                row = group * GROUP + slot
-                for kind in range(3):
-                    own_rows[kind, row : row + 1] = swapped[kind : kind + 1]
-
         wait_near(*stats)
         fill = jnp.where(lax.broadcasted_iota(jnp.int32, (8, 128), 0) == 0, NEG, 0.0)
         for row in range(stretches):
@@ -340,12 +335,12 @@
                 found = jnp.where(jnp.full((8, 128), live, jnp.int32) > 0, stats[1][own_pick[row * 3 + pick]], fill)
                 for kind in range(3):
                     far_rows[pick, kind, row : row + 1] = found[kind : kind + 1]
-        best = own_rows[0]
+        best = own_rows[chunk, 0]
         for pick in range(3):
             best = jnp.maximum(best, far_rows[pick, 0])
-        weight = jnp.exp2((own_rows[0] - best) * EXPO)
-        total = own_rows[1] * weight
-        inner = own_rows[2] * weight
+        weight = jnp.exp2((own_rows[chunk, 0] - best) * EXPO)
+        total = own_rows[chunk, 1] * weight
+        inner = own_rows[chunk, 2] * weight
         for pick in range(3):
             weight = jnp.exp2((far_rows[pick, 0] - best) * EXPO)
             total += far_rows[pick, 1] * weight
@@ -356,14 +351,12 @@
             logs_own[row, 0:1] = log_total[row : row + 1]
             logs_own[row, 1:2] = delta[row : row + 1]
 
-        def send_logs(peer):
+        for peer in range(n - 1):
             row = sent_stretch[peer]
             used = jnp.full((1, 128), sent_used[peer], jnp.int32) > 0
             logs[0][peer, 0:1] = jnp.where(used, logs_own[row, 0:1], BIG)
             logs[0][peer, 1:2] = jnp.where(used, logs_own[row, 1:2], 0.0)
-            pair_copy(*logs, peer, me).start()
-
-        each_near(send_logs)
+        start_down(*logs)
 
         for group in range(stretches // GROUP):
             for kind, kept in ((0, log_head), (1, delta_head)):
@@ -440,9 +433,9 @@
     for chunk in range(last):
         chunk_stats(chunk)
         if chunk + 1 < last:
-            send_rows(g_own, *groups[chunk + 1][1], *chunks[chunk + 1])
+            start_down(*groups[chunk + 1][1])
         if chunk + 2 < last:
-            send_rows(q_ref, *groups[chunk + 2][0], *chunks[chunk + 2])
+            start_down(*groups[chunk + 2][0])
         if chunk > 0:
             chunk_far(chunk - 1)
         chunk_logs(chunk)
@@ -509,7 +502,7 @@
         pltpu.VMEM((heads, block, HD), f32),
         pltpu.VMEM((most, 8, n * QCHUNK), f32),
         pltpu.VMEM((heads, 8, block), f32),
-        pltpu.VMEM((3, stretches, 128), f32),
+        pltpu.VMEM((len(chunks), 3, stretches, 128), f32),
         pltpu.VMEM((3, 3, stretches, 128), f32),
         pltpu.VMEM((stretches, 2, 128), f32),
         pltpu.VMEM((most, 8, n * QCHUNK), f32),

time: 164 us -> 164 us (level)
  Pallas kernels: 155 us -> 153 us
where the time goes in v1:
time: 164 us; the launch traced here: 162 us
  Pallas kernels  153 us (93%)
  local copies, waits for them, and re-layouts  6.13 us (4%)
  other arithmetic  1.99 us (1%)
    pallas_call x1, Pallas kernels, attention_grads(): pl.pallas_call(functools.partial(kernel, n, nh, heads, chunks), out_shape...  153 us
    unnamed x7, local copies, waits for them, and re-layouts  4.69 us

profile of v1, /device:TPU:64, one launch (start us, length us, event | category | flops | bytes accessed | tf_op | source)
XLA Modules:
  0.0 162.1 jit_solution(12051180872739528130)
XLA Ops:
  0.6 0.8 fusion.2
  1.4 0.1 fusion.1
  1.5 0.5 convert_element_type.4.refs_1_
  2.0 0.6 select_reduce_fusion.refs_0_
  2.6 0.1 copy.16
  2.7 0.6 reshape.22.refs_2_
  3.3 0.1 copy.17
  3.4 0.7 reshape.28.refs_3_
  4.1 153.3 %shard_map.76 = (bf16[512,896]{1,0:T(8,128)(2,1)}, bf16[512,896]{1,0:T(8,128)(2,1)}, bf16[512,896]{1,0:T(8,128)(2,1)}) custom-call(s32[32]{0:T(128)} %select_reduce_fusion.refs_0_, s32[32]{0:T(128)} %convert_element_type.4.refs_1_, s32[48]{0:T(128)} %reshape.22.refs_2_, s32[48]{0:T(128)} %reshape.28.refs_3_, bf16[16,32,896]{2,1,0:T(8,128)(2,1)} %bitcast.2, ...), custom_call_target="tpu_custom_call" | custom-call | flops 4932501504 | bytes 6422528 | tf_op jit(solution)/shard_map/pallas_call | solution.py:536
  157.4 0.0 copy-start.1
  157.4 2.3 %copy.21 = bf16[512,896]{1,0:T(8,128)(2,1)} copy(bf16[512,896]{1,0:T(8,128)(2,1)} %get-tuple-element.9) | data formatting | bytes 1835008
  159.6 0.0 copy-done.1
  159.7 0.0 copy-start
  159.7 0.9 copy.22
  160.6 0.6 copy-done
  161.2 0.9 copy.23
  (1 shorter events, 0.0 us)
Async XLA Ops:
  157.4 2.3 %copy-start.1 = (bf16[512,896]{1,0:T(8,128)(2,1)S(1)}, bf16[512,896]{1,0:T(8,128)(2,1)}, u32[]{:S(2)}) copy-start(bf16[512,896]{1,0:T(8,128)(2,1)} %get-tuple-element.10) | copy-start | bytes 2752516
  159.7 1.5 copy-start

commit v2 on v1

--- a/solution.py
+++ b/solution.py
@@ -94,14 +94,15 @@
 
 def kernel(n, nh, heads, chunks, *refs):
     refs = list(refs)
-    sent_stretch, sent_used, own_pick, own_live = refs[:4]
-    q_ref, k_ref, v_ref, g_ref = refs[4:8]
-    dq_ref, dk_ref, dv_ref = refs[8:11]
-    g_own, k_t, dk_acc, dv_acc, dq_own = refs[11:16]
-    stat_far, stat_own, own_rows, far_rows, logs_own, log_far, delta_far, log_head, delta_head = refs[16:25]
-    head_send, head_recv = refs[25:27]
-    far_kept, high_kept, low_kept = refs[27:30], refs[30:33], refs[33:36]
-    rest = refs[36:]
+    sent_code, own_list = refs[:2]
+    refs = refs[2:]
+    q_ref, k_ref, v_ref, g_ref = refs[:4]
+    dq_ref, dk_ref, dv_ref = refs[4:7]
+    g_own, k_t, dk_acc, dv_acc, dq_own = refs[7:12]
+    stat_far, stat_own, own_rows, far_rows, logs_own, log_far, delta_far, log_head, delta_head = refs[12:21]
+    head_send, head_recv = refs[21:23]
+    far_kept, high_kept, low_kept = refs[23:26], refs[26:29], refs[29:32]
+    rest = refs[32:]
     buffers = []
     for _ in chunks:
         buffers.append(rest[:20])
@@ -184,7 +185,7 @@
 
     def gather_rows(source, kind):
         def body(peer):
-            row = sent_stretch[peer]
+            row = jnp.maximum(sent_code[peer] - 1, 0)
             for (start, stop), group in zip(chunks, groups):
                 for head in range(start, stop):
                     group[kind][0][peer, head - start] = source[row, :, head * HD : head * HD + HD]
@@ -292,6 +293,9 @@
                 for kind in range(3):
                     own_rows[chunk, kind, row : row + 1] = swapped[kind : kind + 1]
 
+    last = len(chunks)
+    low_lanes = lax.broadcasted_iota(jnp.int32, (1, 128), 1) < 64
+
     def chunk_stats(chunk):
         (start, stop), (rows, grads, stats, logs, parts) = chunks[chunk], groups[chunk]
         count = stop - start
@@ -318,7 +322,10 @@
             lanes = pl.ds(pl.multiple_of(group * 128, 128), 128)
             held = [stat_far[local, :, lanes] for local in range(count)]
             for slot in range(GROUP):
-                stats[0][group * GROUP + slot] = quarter_swap(held, slot)
+                swapped = quarter_swap(held, slot)
+                moved = pltpu.roll(swapped, 64, 1)
+                stats[0][group * GROUP + slot, 0:1] = jnp.where(low_lanes, swapped[0:1], moved[1:2])
+                stats[0][group * GROUP + slot, 1:2] = swapped[2:3]
             return carry
 
         lax.fori_loop(first_tile * (TILE // 128), n // GROUP, far_swap, 0)
@@ -328,13 +335,15 @@
         (start, stop), (rows, grads, stats, logs, parts) = chunks[chunk], groups[chunk]
         count = stop - start
         wait_near(*stats)
-        fill = jnp.where(lax.broadcasted_iota(jnp.int32, (8, 128), 0) == 0, NEG, 0.0)
+        fill = jnp.where(low_lanes, NEG, 0.0)
         for row in range(stretches):
             for pick in range(3):
-                live = own_live[row * 3 + pick]
-                found = jnp.where(jnp.full((8, 128), live, jnp.int32) > 0, stats[1][own_pick[row * 3 + pick]], fill)
-                for kind in range(3):
-                    far_rows[pick, kind, row : row + 1] = found[kind : kind + 1]
+                source = own_list[row * 3 + pick]
+                live = jnp.full((1, 128), source, jnp.int32) != me
+                far_rows[pick, 0, row : row + 1] = jnp.where(live, stats[1][source, 0:1], fill)
+                far_rows[pick, 2, row : row + 1] = jnp.where(live, stats[1][source, 1:2], 0.0)
+        for pick in range(3):
+            far_rows[pick, 1] = pltpu.roll(far_rows[pick, 0], 64, 1)
         best = own_rows[chunk, 0]
         for pick in range(3):
             best = jnp.maximum(best, far_rows[pick, 0])
@@ -352,8 +361,8 @@
             logs_own[row, 1:2] = delta[row : row + 1]
 
         for peer in range(n - 1):
-            row = sent_stretch[peer]
-            used = jnp.full((1, 128), sent_used[peer], jnp.int32) > 0
+            row = jnp.maximum(sent_code[peer] - 1, 0)
+            used = jnp.full((1, 128), sent_code[peer], jnp.int32) > 0
             logs[0][peer, 0:1] = jnp.where(used, logs_own[row, 0:1], BIG)
             logs[0][peer, 1:2] = jnp.where(used, logs_own[row, 1:2], 0.0)
         start_down(*logs)
@@ -429,7 +438,6 @@
         lax.fori_loop(first_tile, tiles, far_grads, 0)
         start_up(*parts)
 
-    last = len(chunks)
     for chunk in range(last):
         chunk_stats(chunk)
         if chunk + 1 < last:
@@ -472,8 +480,9 @@
             for local in range(stop - start):
                 total = dq_own[start + local, place]
                 for pick in range(3):
-                    live = jnp.full((QCHUNK, HD), own_live[row * 3 + pick], jnp.int32) > 0
-                    far = parts[1][own_pick[row * 3 + pick], local].astype(jnp.float32)
+                    source = own_list[row * 3 + pick]
+                    live = jnp.full((QCHUNK, HD), source, jnp.int32) != me
+                    far = parts[1][source, local].astype(jnp.float32)
                     total += jnp.where(live, far, 0.0)
                 dq_ref[place, pl.ds((start + local) * HD, HD)] = total.astype(jnp.bfloat16)
             return carry
@@ -524,7 +533,7 @@
         for shape, dtype in (
             (row_shape, bf),
             (row_shape, bf),
-            ((n, 8, 128), f32),
+            ((n, 2, 128), f32),
             ((n, 2, 128), f32),
             (row_shape, bf),
         ):
@@ -536,7 +545,7 @@
     return pl.pallas_call(
         functools.partial(kernel, n, nh, heads, chunks),
         out_shape=(out, out, out),
-        in_specs=[small] * 4 + [whole] * 4,
+        in_specs=[small] * 2 + [whole] * 4,
         out_specs=(whole, whole, whole),
         scratch_shapes=scratch,
         cost_estimate=pl.CostEstimate(flops=14 * pairs, bytes_accessed=14 * block * feats, transcendentals=0),
@@ -552,18 +561,9 @@
     me = lax.axis_index("seq")
     stretches = queries.shape[0] // QCHUNK
     own = lax.dynamic_slice_in_dim(selection, me * stretches, stretches, 0)
-    live = own != me
-    peers = jnp.arange(n, dtype=jnp.int32)
-    hits = (own[:, :, None] == peers[None, None, :]) & live[:, :, None]
-    places = jnp.arange(stretches, dtype=jnp.int32)[:, None, None]
-    used = jnp.any(hits, axis=(0, 1)).astype(jnp.int32)
-    stretch = jnp.sum(jnp.where(hits, places, 0), axis=(0, 1))
-    tables = (
-        stretch,
-        used,
-        jnp.where(live, own, 0).reshape(-1),
-        live.astype(jnp.int32).reshape(-1),
-    )
+    hits = (own[:, :, None] == jnp.arange(n, dtype=jnp.int32)) & (own != me)[:, :, None]
+    places = jnp.arange(1, stretches + 1, dtype=jnp.int32)[:, None, None]
+    tables = (jnp.sum(jnp.where(hits, places, 0), axis=(0, 1)), own.reshape(-1))
     return attention_grads(n, nh, tables, queries, keys, values, out_grad)
 
 

time: 164 us -> 160 us (0.976)
  Pallas kernels: 153 us -> 151 us
    pallas_call x1, Pallas kernels: 153 us -> 151 us  [attention_grads(): pl.pallas_call(functools.partial(kernel, n, nh, heads, chunks), out_shape...]
where the time goes in v2:
time: 160 us; the launch traced here: 158 us
  Pallas kernels  151 us (94%)
  local copies, waits for them, and re-layouts  5.38 us (3%)
    pallas_call x1, Pallas kernels, attention_grads(): pl.pallas_call(functools.partial(kernel, n, nh, heads, chunks), out_shape...  151 us
    unnamed x7, local copies, waits for them, and re-layouts  4.69 us

profile of v2, /device:TPU:64, one launch (start us, length us, event | category | flops | bytes accessed | tf_op | source)
XLA Modules:
  0.0 158.4 jit_solution(13978609342428598131)
XLA Ops:
  0.6 0.8 broadcast_compare_fusion
  1.4 0.6 select_reduce_fusion.refs_0_
  2.0 0.1 copy.14
  2.1 0.6 reshape.21.refs_1_
  2.7 151.0 %shard_map.76 = (bf16[512,896]{1,0:T(8,128)(2,1)}, bf16[512,896]{1,0:T(8,128)(2,1)}, bf16[512,896]{1,0:T(8,128)(2,1)}) custom-call(s32[32]{0:T(128)} %select_reduce_fusion.refs_0_, s32[48]{0:T(128)} %reshape.21.refs_1_, bf16[16,32,896]{2,1,0:T(8,128)(2,1)} %bitcast.2, bf16[512,896]{1,0:T(8,128)(2,1)} %refs_3_.1, bf16[512,896]{1,0:T(8,128)(2,1)} %refs_4_.1, ...), custom_call_target="tpu_custom_call" | custom-call | flops 4932501504 | bytes 6422528 | tf_op jit(solution)/shard_map/pallas_call | solution.py:545
  153.7 0.0 copy-start.1
  153.7 2.3 %copy.18 = bf16[512,896]{1,0:T(8,128)(2,1)} copy(bf16[512,896]{1,0:T(8,128)(2,1)} %get-tuple-element.8) | data formatting | bytes 1835008
  156.0 0.0 copy-done.1
  156.0 0.0 copy-start
  156.0 0.9 copy.19
  156.9 0.6 copy-done
  157.5 0.9 copy.20
  (1 shorter events, 0.0 us)
Async XLA Ops:
  153.7 2.3 %copy-start.1 = (bf16[512,896]{1,0:T(8,128)(2,1)S(1)}, bf16[512,896]{1,0:T(8,128)(2,1)}, u32[]{:S(2)}) copy-start(bf16[512,896]{1,0:T(8,128)(2,1)} %get-tuple-element.9) | copy-start | bytes 2752516
  156.0 1.5 copy-start

commit v3 on v2

--- a/solution.py
+++ b/solution.py
@@ -436,27 +436,19 @@
             return carry
 
         lax.fori_loop(first_tile, tiles, far_grads, 0)
-        start_up(*parts)
 
     for chunk in range(last):
         chunk_stats(chunk)
         if chunk + 1 < last:
             start_down(*groups[chunk + 1][1])
+        if chunk > 0:
+            chunk_far(chunk - 1)
+        chunk_logs(chunk)
         if chunk + 2 < last:
             start_down(*groups[chunk + 2][0])
         if chunk > 0:
-            chunk_far(chunk - 1)
-        chunk_logs(chunk)
+            start_up(*groups[chunk - 1][4])
         chunk_own(chunk)
-    chunk_far(last - 1)
-
-    def write_keys(head, carry):
-        cols = head_cols(head)
-        dk_ref[:, cols] = dk_acc[head].astype(jnp.bfloat16)
-        dv_ref[:, cols] = (dv_acc[head] * math.sqrt(HD)).astype(jnp.bfloat16)
-        return carry
-
-    lax.fori_loop(0, heads, write_keys, 0)
 
     def all_sent():
         def head_sent(step, carry):
@@ -489,8 +481,18 @@
 
         lax.fori_loop(0, stretches, write_queries, 0)
 
-    for chunk in range(last - 1):
+    def write_keys(head, carry):
+        cols = head_cols(head)
+        dk_ref[:, cols] = dk_acc[head].astype(jnp.bfloat16)
+        dv_ref[:, cols] = (dv_acc[head] * math.sqrt(HD)).astype(jnp.bfloat16)
+        return carry
+
+    for chunk in range(last - 2):
         chunk_queries(chunk)
+    chunk_far(last - 1)
+    start_up(*groups[last - 1][4])
+    lax.fori_loop(0, heads, write_keys, 0)
+    chunk_queries(last - 2)
     all_sent()
     chunk_queries(last - 1)
 

time: 160 us -> 159 us (level); the launches traced: 158 us -> 159 us
  no operation moved by 1% of the time
where the time goes in v3:
time: 159 us
  Pallas kernels  152 us (96%)
  local copies, waits for them, and re-layouts  5.38 us (3%)
    pallas_call x1, Pallas kernels, attention_grads(): pl.pallas_call(functools.partial(kernel, n, nh, heads, chunks), out_shape...  152 us
    unnamed x7, local copies, waits for them, and re-layouts  4.69 us

profile of v3, /device:TPU:64, one launch (start us, length us, event | category | flops | bytes accessed | tf_op | source)
XLA Modules:
  0.0 159.2 jit_solution(1159123665183271862)
XLA Ops:
  0.6 0.8 broadcast_compare_fusion
  1.4 0.6 select_reduce_fusion.refs_0_
  2.0 0.1 copy.14
  2.1 0.6 reshape.21.refs_1_
  2.7 151.8 %shard_map.76 = (bf16[512,896]{1,0:T(8,128)(2,1)}, bf16[512,896]{1,0:T(8,128)(2,1)}, bf16[512,896]{1,0:T(8,128)(2,1)}) custom-call(s32[32]{0:T(128)} %select_reduce_fusion.refs_0_, s32[48]{0:T(128)} %reshape.21.refs_1_, bf16[16,32,896]{2,1,0:T(8,128)(2,1)} %bitcast.2, bf16[512,896]{1,0:T(8,128)(2,1)} %refs_3_.1, bf16[512,896]{1,0:T(8,128)(2,1)} %refs_4_.1, ...), custom_call_target="tpu_custom_call" | custom-call | flops 4932501504 | bytes 6422528 | tf_op jit(solution)/shard_map/pallas_call | solution.py:547
  154.5 0.0 copy-start.1
  154.6 2.3 %copy.18 = bf16[512,896]{1,0:T(8,128)(2,1)} copy(bf16[512,896]{1,0:T(8,128)(2,1)} %get-tuple-element.8) | data formatting | bytes 1835008
  156.8 0.0 copy-done.1
  156.8 0.0 copy-start
  156.8 0.9 copy.19
  157.7 0.6 copy-done
  158.3 0.9 copy.20
  (1 shorter events, 0.0 us)
Async XLA Ops:
  154.5 2.3 %copy-start.1 = (bf16[512,896]{1,0:T(8,128)(2,1)S(1)}, bf16[512,896]{1,0:T(8,128)(2,1)}, u32[]{:S(2)}) copy-start(bf16[512,896]{1,0:T(8,128)(2,1)} %get-tuple-element.9) | copy-start | bytes 2752516
  156.8 1.5 copy-start

commit v4 on v3

--- a/solution.py
+++ b/solution.py
@@ -256,6 +256,7 @@
 
     lax.fori_loop(1, nh, wait_head, 0)
     gather_rows(g_own, 1)
+    start_down(*groups[1][1])
 
     half = block // 2
     middle = stretches // 2
@@ -439,14 +440,16 @@
 
     for chunk in range(last):
         chunk_stats(chunk)
-        if chunk + 1 < last:
-            start_down(*groups[chunk + 1][1])
+        if chunk > 1:
+            start_up(*groups[chunk - 2][4])
+        if chunk + 2 < last:
+            start_down(*groups[chunk + 2][0])
         if chunk > 0:
             chunk_far(chunk - 1)
         chunk_logs(chunk)
         if chunk + 2 < last:
-            start_down(*groups[chunk + 2][0])
-        if chunk > 0:
+            start_down(*groups[chunk + 2][1])
+        if chunk == last - 1:
             start_up(*groups[chunk - 1][4])
         chunk_own(chunk)
 

time: 159 us -> 157 us (0.987)
  Pallas kernels: 152 us -> 149 us
    pallas_call x1, Pallas kernels: 152 us -> 149 us  [attention_grads(): pl.pallas_call(functools.partial(kernel, n, nh, heads, chunks), out_shape...]
where the time goes in v4:
time: 157 us
  Pallas kernels  149 us (95%)
  local copies, waits for them, and re-layouts  5.38 us (3%)
    pallas_call x1, Pallas kernels, attention_grads(): pl.pallas_call(functools.partial(kernel, n, nh, heads, chunks), out_shape...  149 us
    unnamed x7, local copies, waits for them, and re-layouts  4.69 us

profile of v4, /device:TPU:64, one launch (start us, length us, event | category | flops | bytes accessed | tf_op | source)
XLA Modules:
  0.0 156.8 jit_solution(9942213054577985752)
XLA Ops:
  0.6 0.8 broadcast_compare_fusion
  1.4 0.6 select_reduce_fusion.refs_0_
  2.0 0.1 copy.14
  2.1 0.6 reshape.21.refs_1_
  2.7 149.4 %shard_map.76 = (bf16[512,896]{1,0:T(8,128)(2,1)}, bf16[512,896]{1,0:T(8,128)(2,1)}, bf16[512,896]{1,0:T(8,128)(2,1)}) custom-call(s32[32]{0:T(128)} %select_reduce_fusion.refs_0_, s32[48]{0:T(128)} %reshape.21.refs_1_, bf16[16,32,896]{2,1,0:T(8,128)(2,1)} %bitcast.2, bf16[512,896]{1,0:T(8,128)(2,1)} %refs_3_.1, bf16[512,896]{1,0:T(8,128)(2,1)} %refs_4_.1, ...), custom_call_target="tpu_custom_call" | custom-call | flops 4932501504 | bytes 6422528 | tf_op jit(solution)/shard_map/pallas_call | solution.py:550
  152.1 0.0 copy-start.1
  152.1 2.3 %copy.18 = bf16[512,896]{1,0:T(8,128)(2,1)} copy(bf16[512,896]{1,0:T(8,128)(2,1)} %get-tuple-element.8) | data formatting | bytes 1835008
  154.4 0.0 copy-done.1
  154.4 0.0 copy-start
  154.4 0.9 copy.19
  155.3 0.6 copy-done
  155.9 0.9 copy.20
  (1 shorter events, 0.0 us)
Async XLA Ops:
  152.1 2.3 %copy-start.1 = (bf16[512,896]{1,0:T(8,128)(2,1)S(1)}, bf16[512,896]{1,0:T(8,128)(2,1)}, u32[]{:S(2)}) copy-start(bf16[512,896]{1,0:T(8,128)(2,1)} %get-tuple-element.9) | copy-start | bytes 2752516
  154.4 1.5 copy-start
